TPU v7x, 256 devices: a whole 4x4x8 slice. The times are simulated.
256 devices in a mesh: head: 8 (over x, y_hi), ctx: 32 (over z, y_lo, core).
Axes of the slice: x: 4, y: 4 (y_hi: 2, y_lo: 2; y = y_hi * 2 + y_lo), z: 8, core: 2. Of those that a mesh axis runs over, the one named last changes fastest.
Arguments:
- queries: bfloat16 [8192, 1024], P('ctx', 'head'), may hold values from -6 to 6
- keys: bfloat16 [8192, 1024], P('ctx', 'head'), may hold values from -6 to 6
- values: bfloat16 [8192, 1024], P('ctx', 'head'), may hold values from -6 to 6
- teacher_rows: bfloat16 [12288, 1024], P(('head', 'ctx')), may hold values from -3 to 3
- slots: int32 [12288], P(('head', 'ctx')), may hold values from 0 to 95, as said below
- spans: int32 [12288, 2], P(('head', 'ctx')), may hold values from 0 to 256, as said below
Outputs:
- grad_queries: bfloat16 [8192, 1024], P('ctx', 'head')
- grad_keys: bfloat16 [8192, 1024], P('ctx', 'head')
- grad_values: bfloat16 [8192, 1024], P('ctx', 'head')
Inputs may be any that keep to these rules, and one draw needn't show every extreme that they name: `slots`: in each block of 48 rows (the rows of one device) the values are distinct, so no block has more than 3 rows whose value // 3 is the same; in every draw one index of ctx gets exactly 3 rows from every block. `spans`: each span lies within the 256 student tokens of its index of ctx and covers 1 to 8 of them; some span covers exactly 8 and some ends at 256.
All inputs are finite; a program needn't handle non-finite values.
Results may differ from a plain program's by a relative error of at most 0.0076.
Values may be sent and summed in bfloat16 or wider, within the bound.
A program may use at most 64 MiB of HBM per device.

v0:
```python
import functools
import math

import jax
import jax.numpy as jnp
from jax import lax
from jax.experimental import pallas as pl
from jax.experimental.pallas import tpu as pltpu
from jax.sharding import PartitionSpec as P

DH = 128
CAP = 3
GROUP = 8
CHUNK = 512
MASKED = -1e30
MESH = pl.DeviceIdType.MESH
F32 = jnp.float32
BF16 = jnp.bfloat16


def dot_nt(a, b):
    return lax.dot_general(a, b, (((1,), (1,)), ((), ())), preferred_element_type=F32)


def dot_nn(a, b):
    return lax.dot_general(a, b, (((1,), (0,)), ((), ())), preferred_element_type=F32)


def iota(shape, dim):
    return lax.broadcasted_iota(jnp.int32, shape, dim)


def kernel(heads, ctxs, group, *refs):
    (q_hbm, k_hbm, v_hbm, t_hbm, slots_hbm, spans_hbm, out_ref) = refs[:7]
    (slots_in, spans_in, hop1_in, hop2_out, hop2_in) = refs[7:12]
    (qg, dog, kb, vb, kt, pt, p16, dp, mrow, lse_st, del_st, drow) = refs[12:24]
    (dqa, dq_out, dq_in, dk_out, dk_in, dk_own, dv_out, dv_in, dv_own) = refs[24:33]
    (dk_part, dk_land, dk_keep, dv_part, dv_land, dv_keep, out_v) = refs[33:40]
    (in_sem, h_send, h_recv, c_send, c_recv, q_send, q_recv, do_send, do_recv) = refs[40:49]
    (l_send, l_recv, d_send, d_recv, dq_send, dq_recv) = refs[49:55]
    (k_send, k_recv, v_send, v_recv, kn_send, kn_recv, vn_send, vn_recv) = refs[55:63]
    (pv_send, pv_recv, pk_send, pk_recv, dk_send, dk_recv, dv_send, dv_recv) = refs[63:]
    me_h = lax.axis_index("head")
    me_c = lax.axis_index("ctx")
    z = lax.div(me_c, group)
    r = lax.rem(me_c, group)
    base = z * group
    core = lax.rem(r, 2)
    chip = lax.div(r, 2)
    chips = group // 2
    sibling = r + 1 - 2 * core
    rows = q_hbm.shape[0]
    trows = t_hbm.shape[0]
    lines = ctxs // group
    chunks = chips * rows // CHUNK
    per_chunk = CHUNK // rows
    other = 1 - core
    scale = 1.0 / math.sqrt(DH)

    def each(start, stop, f):
        def body(i, carry):
            f(i)
            return carry

        lax.fori_loop(start, stop, body, 0)

    def every(start, stop, f):
        for i in range(start, stop):
            f(i)

    def mate(i):
        return lax.rem(chip + i, chips)

    def device(of_chip):
        return (me_h, base + 2 * of_chip + core)

    def block(index):
        return pl.ds(pl.multiple_of(index * rows, rows), rows)

    def remote(src, dst, send, recv, device):
        return pltpu.make_async_remote_copy(
            src_ref=src,
            dst_ref=dst,
            send_sem=send,
            recv_sem=recv,
            device_id=device,
            device_id_type=MESH,
        )

    def hop1(i):
        peer = lax.rem(me_h + i, heads)
        columns = pl.ds(pl.multiple_of(peer * DH, DH), DH)
        return [
            remote(src, dst, h_send, sem, (peer, me_c))
            for src, dst, sem in (
                (slots_hbm, slots_in.at[me_h], h_recv.at[0]),
                (spans_hbm, spans_in.at[me_h], h_recv.at[1]),
                (t_hbm.at[:, columns], hop1_in.at[me_h, pl.ds(0, trows), :], h_recv.at[2]),
            )
        ]

    def hop1_all():
        most = pl.ds(0, heads - 1)
        here = (
            slots_in.at[most],
            spans_in.at[most],
            hop1_in.at[most, pl.ds(0, trows), :],
        )
        return [
            remote(ref, ref, h_send, h_recv.at[j], (me_h, me_c)) for j, ref in enumerate(here)
        ]

    def hop2(i):
        peer = lax.rem(me_c + i, ctxs)
        return remote(hop2_out.at[peer], hop2_in.at[me_c], c_send, c_recv, (me_h, peer))

    def hop2_all():
        most = pl.ds(0, ctxs - 1)
        return remote(hop2_out.at[most], hop2_in.at[most], c_send, c_recv, (me_h, me_c))

    def share_start(buffer, send, recv):
        here = buffer.at[block(chip), :]
        every(1, chips, lambda i: remote(here, here, send, recv, device(mate(i))).start())

    def share_all(buffer, send, recv):
        most = buffer.at[pl.ds(0, (chips - 1) * rows), :]
        return remote(most, most, send, recv, (me_h, me_c))

    def to_line(buffer, send, recv, line):
        here = buffer.at[z, core]
        return remote(here, here, send.at[line], recv.at[z], (me_h, line * group + r))

    def from_line(buffer, send, recv, line):
        here = buffer.at[line, core]
        return remote(here, here, send.at[line], recv.at[line], (me_h, line * group + r))

    def near(buffer, send, recv, line):
        here = buffer.at[line, core]
        return remote(here, here, send.at[line], recv.at[line], (me_h, base + sibling))

    def near_arrival(buffer, send, recv, line):
        here = buffer.at[line, other]
        return remote(here, here, send.at[line], recv.at[line], (me_h, base + sibling))

    def forward(buffer, send, recv, near_send, near_recv):
        def step(line):
            from_line(buffer, send, recv, line).wait_recv()
            near(buffer, near_send, near_recv, line).start()

        each(0, z, step)

    def part(out, landing, send, recv, line):
        return remote(
            out.at[line], landing.at[line], send.at[line], recv.at[line], (me_h, base + sibling)
        )

    def stat(buffer, send, recv, i):
        return remote(buffer.at[chip], buffer.at[chip], send, recv, device(mate(i)))

    def stat_all(buffer, send, recv):
        most = buffer.at[pl.ds(0, chips - 1)]
        return remote(most, most, send, recv, (me_h, me_c))

    def back(out, landing, send, recv, line):
        return remote(
            out.at[line], landing.at[z], send.at[line], recv.at[z], (me_h, line * group + r)
        )

    def back_arrival(out, landing, send, recv, line):
        return remote(
            out.at[line], landing.at[line], send.at[line], recv.at[line], (me_h, line * group + r)
        )

    def dq_away(i):
        return remote(
            dq_out.at[mate(i)], dq_in.at[chip], dq_send.at[i], dq_recv.at[chip], device(mate(i))
        )

    def dq_arrival(i):
        return remote(
            dq_out.at[mate(i)], dq_in.at[mate(i)], dq_send.at[i], dq_recv.at[mate(i)], device(mate(i))
        )

    def out_copy(which):
        return pltpu.make_async_copy(out_v.at[which], out_ref.at[which], in_sem.at[6 + which])

    barrier = pltpu.get_barrier_semaphore()

    def greet(device):
        pl.semaphore_signal(barrier, inc=1, device_id=device, device_id_type=MESH)

    loads = [
        pltpu.make_async_copy(q_hbm, qg.at[block(chip), :], in_sem.at[0]),
        pltpu.make_async_copy(k_hbm, kb.at[z, core], in_sem.at[1]),
        pltpu.make_async_copy(v_hbm, vb.at[z, core], in_sem.at[2]),
        pltpu.make_async_copy(slots_hbm, slots_in.at[me_h], in_sem.at[3]),
        pltpu.make_async_copy(spans_hbm, spans_in.at[me_h], in_sem.at[4]),
        pltpu.make_async_copy(
            t_hbm.at[:, pl.ds(pl.multiple_of(me_h * DH, DH), DH)],
            hop1_in.at[me_h, pl.ds(0, trows), :],
            in_sem.at[5],
        ),
    ]
    every(1, heads, lambda i: greet((lax.rem(me_h + i, heads), me_c)))
    every(1, ctxs, lambda i: greet((me_h, lax.rem(me_c + i, ctxs))))
    for load in loads:
        load.start()
    hop1_in[:, trows:64, :] = jnp.zeros((heads, 64 - trows, DH), BF16)

    pl.semaphore_wait(barrier, heads - 1 + ctxs - 1)

    def hop1_start(i):
        for copy in hop1(i):
            copy.start()

    every(1, heads, hop1_start)
    for load in loads:
        load.wait()
    share_start(qg, q_send, q_recv)
    each(z + 1, lines, lambda line: to_line(kb, k_send, k_recv, line).start())
    near(kb, kn_send, kn_recv, z).start()
    near(vb, vn_send, vn_recv, z).start()
    for copy in hop1_all():
        copy.wait_recv()

    kdepth = heads * 64
    teacher = hop1_in[...].reshape(kdepth, DH)
    eye = iota((64, trows), 0) == iota((64, trows), 1)
    ones = jnp.ones((trows, DH), BF16)
    firsts, lasts = [], []
    slots = jnp.zeros((16, trows), F32)
    for h in range(heads):
        spans = spans_in[h].astype(F32)
        firsts.append(jnp.where(eye, spans[0:1], 0.0).astype(BF16))
        lasts.append(jnp.where(eye, spans[1:2], 0.0).astype(BF16))
        slots = jnp.where(iota((16, trows), 0) == h, slots_in[h].astype(F32), slots)
    first = dot_nn(jnp.concatenate(firsts, axis=0), ones).astype(BF16)
    last = dot_nn(jnp.concatenate(lasts, axis=0), ones).astype(BF16)
    place = jnp.bitwise_and(iota((trows, DH), 1), 63)
    pick = (place == iota((trows, DH), 0)).astype(F32).astype(BF16)
    slots = dot_nn(slots.astype(BF16), pick) + 128.0 * iota((16, DH), 0).astype(F32)
    unused = jnp.bitwise_and(iota((16, DH), 1), 63) >= trows
    slots = jnp.where(unused, -1.0, slots)
    left = iota((1, DH), 1) < 64
    codes = [
        jnp.where(left, slots[h : h + 1], slots[h + 1 : h + 2]) for h in range(0, heads, 2)
    ]
    mine = lax.rem(me_c, 4) * 32

    def pack(step):
        row = iota((256, DH), 0)
        within = jnp.bitwise_and(row, 31)
        dest = lax.shift_right_logical(row, 5) + step * 8
        spot = lax.div(within, heads)
        head = within - spot * heads
        wanted = jnp.where(spot < CAP, dest * CAP + spot + 128 * head, -5).astype(F32)
        chosen = [(wanted == code).astype(F32).astype(BF16) for code in codes]
        chosen = jnp.concatenate(chosen, axis=1)
        moved = dot_nn(chosen, teacher).reshape(8, 32, DH)
        diagonal = (iota((256, DH), 1) == within + mine).astype(F32)
        lower = (dot_nn(chosen, first) * diagonal).reshape(8, 32, DH)
        upper = (dot_nn(chosen, last) * diagonal).reshape(8, 32, DH)
        lower = jnp.sum(lower, axis=1, keepdims=True)
        upper = jnp.sum(upper, axis=1, keepdims=True)
        line = iota((8, 8, DH), 1)
        tail = jnp.where(line == 0, lower, jnp.where(line == 1, upper, 0.0))
        message = jnp.concatenate([moved[:, 0:24, :], tail], axis=1)
        hop2_out[pl.ds(step * 8, 8)] = message.astype(BF16)

    for step in range(ctxs // 8):
        pack(step)
    every(1, ctxs, lambda i: hop2(i).start())
    hop2_in[me_c] = hop2_out[me_c]

    each(z + 1, lines, lambda line: to_line(vb, v_send, v_recv, line).start())
    forward(kb, k_send, k_recv, kn_send, kn_recv)
    share_all(qg, q_send, q_recv).wait_recv()

    def transpose_keys(line):
        near_arrival(kb, kn_send, kn_recv, line).wait_recv()
        for side in range(2):
            kt[line, side] = kb[line, side].astype(F32).T.astype(BF16)

    each(0, z + 1, transpose_keys)

    def scores_chunk(qc):
        queries = qg[pl.ds(pl.multiple_of(qc * CHUNK, CHUNK), CHUNK), :]

        def score(line, top):
            for side in range(2):
                s = dot_nt(kb[line, side], queries)
                pt[line, side, qc] = s
                top = jnp.maximum(top, jnp.max(s, axis=0, keepdims=True))
            return top

        top = lax.fori_loop(0, z, score, jnp.full((1, CHUNK), MASKED, F32))
        place = iota((rows, CHUNK), 1) + qc * CHUNK
        query_pos = place + (lax.div(place, rows) + core) * rows
        for side in range(2):
            s = dot_nt(kb[z, side], queries)
            key_pos = iota((rows, CHUNK), 0) + (2 * chip + side) * rows
            s = jnp.where(key_pos <= query_pos, s, MASKED)
            pt[z, side, qc] = s
            top = jnp.maximum(top, jnp.max(s, axis=0, keepdims=True))

        def weight(line, total):
            for side in range(2):
                p = jnp.exp((pt[line, side, qc] - top) * scale)
                pt[line, side, qc] = p
                total = total + jnp.sum(p, axis=0, keepdims=True)
            return total

        total = lax.fori_loop(0, z + 1, weight, jnp.zeros((1, CHUNK), F32))
        mrow[qc] = top * scale
        lse_st[chip, qc] = top * scale + jnp.log(total)

    each(0, chunks, scores_chunk)
    every(1, chips, lambda i: stat(lse_st, l_send, l_recv, i).start())
    stat_all(lse_st, l_send, l_recv).wait_recv()

    def probs_chunk(qc):
        parts = lse_st[:, qc]
        top = jnp.max(parts, axis=0)
        lse = top + jnp.log(jnp.sum(jnp.exp(parts - top[None]), axis=0))
        fade = jnp.exp(mrow[qc] - lse)

        def fix(line):
            for side in range(2):
                prob = pt[line, side, qc] * fade
                pt[line, side, qc] = prob
                p16[line, side, qc] = prob.astype(BF16)

        each(0, z + 1, fix)

    each(0, chunks, probs_chunk)

    hop2_all().wait_recv()
    token = iota((rows, DH), 0).astype(F32)

    def cover(step, total):
        four = hop2_in[pl.ds(step * 4, 4)]
        edges = jnp.sum(four[:, 16:32, :].astype(F32), axis=0)
        lower = edges[8:9]
        upper = edges[9:10]
        covered = jnp.where((token >= lower) & (token < upper), 1.0, 0.0).astype(BF16)
        return total + dot_nn(covered, four.reshape(4 * 32, DH))

    grad = jnp.zeros((rows, DH), F32)
    for step in range(ctxs // 4):
        grad = cover(step, grad)
    dog[block(chip), :] = grad.astype(BF16)
    share_start(dog, do_send, do_recv)

    forward(vb, v_send, v_recv, vn_send, vn_recv)
    share_all(dog, do_send, do_recv).wait_recv()

    def value_terms(line, side):
        total = jnp.zeros((rows, DH), F32)
        for qc in range(chunks):
            total += dot_nn(p16[line, side, qc], dog[qc * CHUNK : (qc + 1) * CHUNK, :])
        return total

    def value_parts(line):
        dv_part[line] = value_terms(line, other).astype(BF16)
        part(dv_part, dv_land, pv_send, pv_recv, line).start()
        dv_keep[line] = value_terms(line, core)

    def value_join(line):
        part(dv_part, dv_land, pv_send, pv_recv, line).wait_recv()
        dv_out[line] = (dv_keep[line] + dv_land[line].astype(F32)).astype(BF16)
        back(dv_out, dv_in, dv_send, dv_recv, line).start()

    each(0, z + 1, value_parts)
    each(0, z, value_join)

    def grad_probs(line, sums):
        for side in range(2):
            for qc in range(chunks):
                d = dot_nt(vb[line, side], dog[qc * CHUNK : (qc + 1) * CHUNK, :])
                dp[line, side, qc] = d
                here = jnp.sum(pt[line, side, qc] * d, axis=0, keepdims=True)
                sums[qc] = here if sums[qc] is None else sums[qc] + here
        return sums

    near_arrival(vb, vn_send, vn_recv, z).wait_recv()
    sums = grad_probs(z, [None] * chunks)
    for qc in range(chunks):
        del_st[chip, qc] = sums[qc]

    def earlier_probs(i):
        line = z - i
        near_arrival(vb, vn_send, vn_recv, line).wait_recv()
        sums = grad_probs(line, [None] * chunks)
        for qc in range(chunks):
            del_st[chip, qc] += sums[qc]

    each(1, z + 1, earlier_probs)
    every(1, chips, lambda i: stat(del_st, d_send, d_recv, i).start())

    for copy in hop1_all():
        copy.wait_send()
    hop2_all().wait_send()
    share_all(qg, q_send, q_recv).wait_send()
    share_all(dog, do_send, do_recv).wait_send()
    stat_all(lse_st, l_send, l_recv).wait_send()

    def lines_sent(line):
        to_line(kb, k_send, k_recv, line).wait_send()
        to_line(vb, v_send, v_recv, line).wait_send()

    each(z + 1, lines, lines_sent)

    def nears_sent(line):
        near(kb, kn_send, kn_recv, line).wait_send()
        near(vb, vn_send, vn_recv, line).wait_send()
        part(dv_part, dv_land, pv_send, pv_recv, line).wait_send()

    each(0, z + 1, nears_sent)
    for j in range(chips):
        dqa[j] = jnp.zeros((DH, rows), F32)

    stat_all(del_st, d_send, d_recv).wait_recv()
    stat_all(del_st, d_send, d_recv).wait_send()

    def deltas(qc):
        drow[qc] = jnp.sum(del_st[:, qc], axis=0)

    each(0, chunks, deltas)

    def dscores(line, side):
        for qc in range(chunks):
            dscore = (pt[line, side, qc] * (dp[line, side, qc] - drow[qc]) * scale).astype(BF16)
            p16[line, side, qc] = dscore
            terms = dot_nn(kt[line, side], dscore)
            for j in range(per_chunk):
                dqa[qc * per_chunk + j] += terms[:, j * rows : (j + 1) * rows]

    def key_terms(line, side):
        total = jnp.zeros((rows, DH), F32)
        for qc in range(chunks):
            total += dot_nn(p16[line, side, qc], qg[qc * CHUNK : (qc + 1) * CHUNK, :])
        return total

    def key_parts(line):
        dk_part[line] = key_terms(line, other).astype(BF16)
        part(dk_part, dk_land, pk_send, pk_recv, line).start()
        dk_keep[line] = key_terms(line, core)

    def key_sum(line):
        part(dk_part, dk_land, pk_send, pk_recv, line).wait_recv()
        return dk_keep[line] + dk_land[line].astype(F32)

    def key_join(line):
        dk_out[line] = key_sum(line).astype(BF16)
        back(dk_out, dk_in, dk_send, dk_recv, line).start()

    def earlier_keys(line):
        dscores(line, other)
        dscores(line, core)
        key_parts(line)
        pl.when(line > 0)(lambda: key_join(line - 1))

    each(0, z, earlier_keys)
    dscores(z, other)
    dscores(z, core)
    dq_out[...] = dqa[...].astype(BF16)
    every(1, chips, lambda i: dq_away(i).start())
    pl.when(z > 0)(lambda: key_join(z - 1))
    key_parts(z)

    part(dv_part, dv_land, pv_send, pv_recv, z).wait_recv()
    dv_own[...] = dv_keep[z] + dv_land[z].astype(F32)

    def dv_add(line):
        back_arrival(dv_out, dv_in, dv_send, dv_recv, line).wait_recv()
        dv_own[...] += dv_in[line].astype(F32)

    each(z + 1, lines, dv_add)
    out_v[2] = dv_own[...].astype(BF16)
    out_copy(2).start()
    dk_own[...] = key_sum(z)

    def dk_add(line):
        back_arrival(dk_out, dk_in, dk_send, dk_recv, line).wait_recv()
        dk_own[...] += dk_in[line].astype(F32)

    each(z + 1, lines, dk_add)
    out_v[1] = dk_own[...].astype(BF16)
    out_copy(1).start()

    def dq_add(i, total):
        dq_arrival(i).wait_recv()
        return total + dq_in[mate(i)].astype(F32)

    dq_total = lax.fori_loop(1, chips, dq_add, dqa[chip])
    out_v[0] = dq_total.T.astype(BF16)
    out_copy(0).start()

    every(1, chips, lambda i: dq_away(i).wait_send())
    each(0, z + 1, lambda line: part(dk_part, dk_land, pk_send, pk_recv, line).wait_send())

    def backs_sent(line):
        back(dv_out, dv_in, dv_send, dv_recv, line).wait_send()
        back(dk_out, dk_in, dk_send, dk_recv, line).wait_send()

    each(0, z, backs_sent)
    for which in range(3):
        out_copy(which).wait()


def shards(heads, ctxs, group, queries, keys, values, teacher_rows, slots, spans):
    rows = queries.shape[0]
    trows = teacher_rows.shape[0]
    lines = ctxs // group
    chips = group // 2
    chunks = chips * rows // CHUNK
    vm = pltpu.VMEM
    dma = pltpu.SemaphoreType.DMA
    parts = [vm((lines, rows, DH), BF16), vm((lines, rows, DH), BF16)]
    scratch = [
        vm((heads, 1, trows), jnp.int32),
        vm((heads, 2, trows), jnp.int32),
        vm((heads, 64, DH), BF16),
        vm((ctxs, 32, DH), BF16),
        vm((ctxs, 32, DH), BF16),
        vm((chips * rows, DH), BF16),
        vm((chips * rows, DH), BF16),
        vm((lines, 2, rows, DH), BF16),
        vm((lines, 2, rows, DH), BF16),
        vm((lines, 2, DH, rows), BF16),
        vm((lines, 2, chunks, rows, CHUNK), F32),
        vm((lines, 2, chunks, rows, CHUNK), BF16),
        vm((lines, 2, chunks, rows, CHUNK), F32),
        vm((chunks, 1, CHUNK), F32),
        vm((chips, chunks, 1, CHUNK), F32),
        vm((chips, chunks, 1, CHUNK), F32),
        vm((chunks, 1, CHUNK), F32),
        vm((chips, DH, rows), F32),
        vm((chips, DH, rows), BF16),
        vm((chips, DH, rows), BF16),
        *parts,
        vm((rows, DH), F32),
        *parts,
        vm((rows, DH), F32),
        *parts,
        vm((lines, rows, DH), F32),
        *parts,
        vm((lines, rows, DH), F32),
        vm((3, rows, DH), BF16),
        dma((9,)),
        dma,
        dma((3,)),
        *([dma] * 10),
        dma((chips,)),
        dma((chips,)),
        *([dma((lines,))] * 16),
    ]
    out = pl.pallas_call(
        functools.partial(kernel, heads, ctxs, group),
        out_shape=jax.ShapeDtypeStruct((3, rows, DH), BF16),
        in_specs=[pl.BlockSpec(memory_space=pl.ANY)] * 6,
        out_specs=pl.BlockSpec(memory_space=pl.ANY),
        scratch_shapes=scratch,
        compiler_params=pltpu.CompilerParams(
            collective_id=0, has_side_effects=True, vmem_limit_bytes=56 * 1024 * 1024
        ),
        name="attention_backward",
    )(queries, keys, values, teacher_rows, slots.reshape(1, trows), spans.T)
    return out[0], out[1], out[2]


def solution(mesh):
    heads, ctxs = mesh.shape["head"], mesh.shape["ctx"]
    group = min(GROUP, ctxs // 2)
    return jax.shard_map(
        functools.partial(shards, heads, ctxs, group),
        mesh=mesh,
        in_specs=(
            P("ctx", "head"),
            P("ctx", "head"),
            P("ctx", "head"),
            P(("head", "ctx"), None),
            P(("head", "ctx")),
            P(("head", "ctx"), None),
        ),
        out_specs=(P("ctx", "head"), P("ctx", "head"), P("ctx", "head")),
        check_vma=False,
    )
```

profile of v0, /device:TPU:37, one launch (start us, length us, event | category | flops | bytes accessed | tf_op | source)
XLA Modules:
  0.0 56.9 jit_solution(3067581555437823420)
XLA Ops:
  0.6 54.7 %attention_backward.1 = bf16[3,256,128]{2,1,0:T(8,128)(2,1)} custom-call(bf16[256,128]{1,0:T(8,128)(2,1)} %refs_0_.1, bf16[256,128]{1,0:T(8,128)(2,1)} %refs_1_.1, bf16[256,128]{1,0:T(8,128)(2,1)} %refs_2_.1, bf16[48,1024]{1,0:T(8,128)(2,1)} %refs_3_.1, s32[1,48]{1,0:T(1,128)} %bitcast.9, s32[2,48]{1,0:T(2,128)} %bitcast.8), custom_call_target="tpu_custom_call" | custom-call | tf_op jit(solution)/shard_map/attention_backward/pallas_call | solution.py:558
  55.3 1.6 %slice_bitcast_fusion = (bf16[256,128]{1,0:T(8,128)(2,1)}, bf16[256,128]{1,0:T(8,128)(2,1)}, bf16[256,128]{1,0:T(8,128)(2,1)}) fusion(bf16[3,256,128]{2,1,0:T(8,128)(2,1)} %attention_backward.1), kind=kLoop, calls=%fused_computation | loop fusion | bytes 393216 | tf_op jit(solution)/shard_map/squeeze | solution.py:569
where the time goes:
time: 57.7 us; the launch traced here: 56.9 us
  Pallas kernels  54.7 us (95%)
  local copies, waits for them, and re-layouts  1.58 us (3%)
  between operations  0.64 us (1%)
    pallas_call x1, Pallas kernels, shards(): pl.pallas_call(functools.partial(kernel, heads, ctxs, group), out_shape=j...  54.7 us
    squeeze x1, local copies, waits for them, and re-layouts, shards(): return (out[0], out[1], out[2])  1.58 us

commit v1 on v0

--- a/solution.py
+++ b/solution.py
@@ -35,11 +35,11 @@
     (slots_in, spans_in, hop1_in, hop2_out, hop2_in) = refs[7:12]
     (qg, dog, kb, vb, kt, pt, p16, dp, mrow, lse_st, del_st, drow) = refs[12:24]
     (dqa, dq_out, dq_in, dk_out, dk_in, dk_own, dv_out, dv_in, dv_own) = refs[24:33]
-    (dk_part, dk_land, dk_keep, dv_part, dv_land, dv_keep, out_v) = refs[33:40]
-    (in_sem, h_send, h_recv, c_send, c_recv, q_send, q_recv, do_send, do_recv) = refs[40:49]
-    (l_send, l_recv, d_send, d_recv, dq_send, dq_recv) = refs[49:55]
-    (k_send, k_recv, v_send, v_recv, kn_send, kn_recv, vn_send, vn_recv) = refs[55:63]
-    (pv_send, pv_recv, pk_send, pk_recv, dk_send, dk_recv, dv_send, dv_recv) = refs[63:]
+    (dk_part, dk_land, dk_keep, dv_part, dv_land, dv_keep) = refs[33:39]
+    (in_sem, h_send, h_recv, c_send, c_recv, q_send, q_recv, do_send, do_recv) = refs[39:48]
+    (l_send, l_recv, d_send, d_recv, dq_send, dq_recv) = refs[48:54]
+    (k_send, k_recv, v_send, v_recv, kn_send, kn_recv, vn_send, vn_recv) = refs[54:62]
+    (pv_send, pv_recv, pk_send, pk_recv, dk_send, dk_recv, dv_send, dv_recv) = refs[62:]
     me_h = lax.axis_index("head")
     me_c = lax.axis_index("ctx")
     z = lax.div(me_c, group)
@@ -180,9 +180,6 @@
         return remote(
             dq_out.at[mate(i)], dq_in.at[mate(i)], dq_send.at[i], dq_recv.at[mate(i)], device(mate(i))
         )
-
-    def out_copy(which):
-        return pltpu.make_async_copy(out_v.at[which], out_ref.at[which], in_sem.at[6 + which])
 
     barrier = pltpu.get_barrier_semaphore()
 
@@ -269,7 +266,8 @@
 
     for step in range(ctxs // 8):
         pack(step)
-    every(1, ctxs, lambda i: hop2(i).start())
+    for i in sorted(range(1, ctxs), key=lambda i: min(i, ctxs - i)):
+        hop2(i).start()
     hop2_in[me_c] = hop2_out[me_c]
 
     each(z + 1, lines, lambda line: to_line(vb, v_send, v_recv, line).start())
@@ -360,18 +358,18 @@
             total += dot_nn(p16[line, side, qc], dog[qc * CHUNK : (qc + 1) * CHUNK, :])
         return total
 
+    def value_join(line):
+        part(dv_part, dv_land, pv_send, pv_recv, line).wait_recv()
+        dv_out[line] = (dv_keep[line] + dv_land[line].astype(F32)).astype(BF16)
+        back(dv_out, dv_in, dv_send, dv_recv, line).start()
+
     def value_parts(line):
         dv_part[line] = value_terms(line, other).astype(BF16)
         part(dv_part, dv_land, pv_send, pv_recv, line).start()
         dv_keep[line] = value_terms(line, core)
-
-    def value_join(line):
-        part(dv_part, dv_land, pv_send, pv_recv, line).wait_recv()
-        dv_out[line] = (dv_keep[line] + dv_land[line].astype(F32)).astype(BF16)
-        back(dv_out, dv_in, dv_send, dv_recv, line).start()
+        pl.when(line > 0)(lambda: value_join(line - 1))
 
     each(0, z + 1, value_parts)
-    each(0, z, value_join)
 
     def grad_probs(line, sums):
         for side in range(2):
@@ -431,7 +429,10 @@
         for qc in range(chunks):
             dscore = (pt[line, side, qc] * (dp[line, side, qc] - drow[qc]) * scale).astype(BF16)
             p16[line, side, qc] = dscore
-            terms = dot_nn(kt[line, side], dscore)
+
+    def query_terms(line):
+        for qc in range(chunks):
+            terms = dot_nn(kt[line, 0], p16[line, 0, qc]) + dot_nn(kt[line, 1], p16[line, 1, qc])
             for j in range(per_chunk):
                 dqa[qc * per_chunk + j] += terms[:, j * rows : (j + 1) * rows]
 
@@ -444,6 +445,8 @@
     def key_parts(line):
         dk_part[line] = key_terms(line, other).astype(BF16)
         part(dk_part, dk_land, pk_send, pk_recv, line).start()
+
+    def key_keeps(line):
         dk_keep[line] = key_terms(line, core)
 
     def key_sum(line):
@@ -456,17 +459,20 @@
 
     def earlier_keys(line):
         dscores(line, other)
+        key_parts(line)
         dscores(line, core)
-        key_parts(line)
+        key_keeps(line)
         pl.when(line > 0)(lambda: key_join(line - 1))
 
     each(0, z, earlier_keys)
     dscores(z, other)
     dscores(z, core)
+    pl.when(z > 0)(lambda: key_join(z - 1))
+    each(0, z + 1, query_terms)
     dq_out[...] = dqa[...].astype(BF16)
     every(1, chips, lambda i: dq_away(i).start())
-    pl.when(z > 0)(lambda: key_join(z - 1))
     key_parts(z)
+    key_keeps(z)
 
     part(dv_part, dv_land, pv_send, pv_recv, z).wait_recv()
     dv_own[...] = dv_keep[z] + dv_land[z].astype(F32)
@@ -476,8 +482,7 @@
         dv_own[...] += dv_in[line].astype(F32)
 
     each(z + 1, lines, dv_add)
-    out_v[2] = dv_own[...].astype(BF16)
-    out_copy(2).start()
+    out_ref[2] = dv_own[...].astype(BF16)
     dk_own[...] = key_sum(z)
 
     def dk_add(line):
@@ -485,16 +490,14 @@
         dk_own[...] += dk_in[line].astype(F32)
 
     each(z + 1, lines, dk_add)
-    out_v[1] = dk_own[...].astype(BF16)
-    out_copy(1).start()
+    out_ref[1] = dk_own[...].astype(BF16)
 
     def dq_add(i, total):
         dq_arrival(i).wait_recv()
         return total + dq_in[mate(i)].astype(F32)
 
     dq_total = lax.fori_loop(1, chips, dq_add, dqa[chip])
-    out_v[0] = dq_total.T.astype(BF16)
-    out_copy(0).start()
+    out_ref[0] = dq_total.T.astype(BF16)
 
     every(1, chips, lambda i: dq_away(i).wait_send())
     each(0, z + 1, lambda line: part(dk_part, dk_land, pk_send, pk_recv, line).wait_send())
@@ -504,8 +507,6 @@
         back(dk_out, dk_in, dk_send, dk_recv, line).wait_send()
 
     each(0, z, backs_sent)
-    for which in range(3):
-        out_copy(which).wait()
 
 
 def shards(heads, ctxs, group, queries, keys, values, teacher_rows, slots, spans):
@@ -546,8 +547,7 @@
         vm((lines, rows, DH), F32),
         *parts,
         vm((lines, rows, DH), F32),
-        vm((3, rows, DH), BF16),
-        dma((9,)),
+        dma((6,)),
         dma,
         dma((3,)),
         *([dma] * 10),
@@ -557,9 +557,9 @@
     ]
     out = pl.pallas_call(
         functools.partial(kernel, heads, ctxs, group),
-        out_shape=jax.ShapeDtypeStruct((3, rows, DH), BF16),
+        out_shape=pltpu.VMEM((3, rows, DH), BF16),
         in_specs=[pl.BlockSpec(memory_space=pl.ANY)] * 6,
-        out_specs=pl.BlockSpec(memory_space=pl.ANY),
+        out_specs=pl.BlockSpec(memory_space=pltpu.VMEM),
         scratch_shapes=scratch,
         compiler_params=pltpu.CompilerParams(
             collective_id=0, has_side_effects=True, vmem_limit_bytes=56 * 1024 * 1024

time: 57.7 us -> 55.8 us (0.967)
  Pallas kernels: 54.7 us -> 53.8 us
  local copies, waits for them, and re-layouts: 1.58 us -> 0.68 us
    squeeze x1, local copies, waits for them, and re-layouts: 1.58 us -> 0.68 us  [shards(): return (out[0], out[1], out[2])]
    pallas_call x1, Pallas kernels: 54.7 us -> 53.8 us  [shards(): pl.pallas_call(functools.partial(kernel, heads, ctxs, group), out_shape=p...]
where the time goes in v1:
time: 55.8 us; the launch traced here: 55.1 us
  Pallas kernels  53.8 us (96%)
  local copies, waits for them, and re-layouts  0.68 us (1%)
  between operations  0.64 us (1%)
    pallas_call x1, Pallas kernels, shards(): pl.pallas_call(functools.partial(kernel, heads, ctxs, group), out_shape=p...  53.8 us

profile of v1, /device:TPU:37, one launch (start us, length us, event | category | flops | bytes accessed | tf_op | source)
XLA Modules:
  0.0 55.1 jit_solution(5161307648926031982)
XLA Ops:
  0.6 53.8 %attention_backward.1 = bf16[3,256,128]{2,1,0:T(8,128)(2,1)S(1)} custom-call(bf16[256,128]{1,0:T(8,128)(2,1)} %refs_0_.1, bf16[256,128]{1,0:T(8,128)(2,1)} %refs_1_.1, bf16[256,128]{1,0:T(8,128)(2,1)} %refs_2_.1, bf16[48,1024]{1,0:T(8,128)(2,1)} %refs_3_.1, s32[1,48]{1,0:T(1,128)} %bitcast.9, s32[2,48]{1,0:T(2,128)} %bitcast.8), custom_call_target="tpu_custom_call" | custom-call | tf_op jit(solution)/shard_map/attention_backward/pallas_call | solution.py:558
  54.4 0.7 %slice_bitcast_fusion = (bf16[256,128]{1,0:T(8,128)(2,1)}, bf16[256,128]{1,0:T(8,128)(2,1)}, bf16[256,128]{1,0:T(8,128)(2,1)}) fusion(bf16[3,256,128]{2,1,0:T(8,128)(2,1)S(1)} %attention_backward.1), kind=kLoop, calls=%fused_computation | loop fusion | bytes 393216 | tf_op jit(solution)/shard_map/squeeze | solution.py:569

commit v2 on v1

--- a/solution.py
+++ b/solution.py
@@ -352,25 +352,6 @@
     forward(vb, v_send, v_recv, vn_send, vn_recv)
     share_all(dog, do_send, do_recv).wait_recv()
 
-    def value_terms(line, side):
-        total = jnp.zeros((rows, DH), F32)
-        for qc in range(chunks):
-            total += dot_nn(p16[line, side, qc], dog[qc * CHUNK : (qc + 1) * CHUNK, :])
-        return total
-
-    def value_join(line):
-        part(dv_part, dv_land, pv_send, pv_recv, line).wait_recv()
-        dv_out[line] = (dv_keep[line] + dv_land[line].astype(F32)).astype(BF16)
-        back(dv_out, dv_in, dv_send, dv_recv, line).start()
-
-    def value_parts(line):
-        dv_part[line] = value_terms(line, other).astype(BF16)
-        part(dv_part, dv_land, pv_send, pv_recv, line).start()
-        dv_keep[line] = value_terms(line, core)
-        pl.when(line > 0)(lambda: value_join(line - 1))
-
-    each(0, z + 1, value_parts)
-
     def grad_probs(line, sums):
         for side in range(2):
             for qc in range(chunks):
@@ -394,6 +375,25 @@
 
     each(1, z + 1, earlier_probs)
     every(1, chips, lambda i: stat(del_st, d_send, d_recv, i).start())
+
+    def value_terms(line, side):
+        total = jnp.zeros((rows, DH), F32)
+        for qc in range(chunks):
+            total += dot_nn(p16[line, side, qc], dog[qc * CHUNK : (qc + 1) * CHUNK, :])
+        return total
+
+    def value_join(line):
+        part(dv_part, dv_land, pv_send, pv_recv, line).wait_recv()
+        dv_out[line] = (dv_keep[line] + dv_land[line].astype(F32)).astype(BF16)
+        back(dv_out, dv_in, dv_send, dv_recv, line).start()
+
+    def value_parts(line):
+        dv_part[line] = value_terms(line, other).astype(BF16)
+        part(dv_part, dv_land, pv_send, pv_recv, line).start()
+        dv_keep[line] = value_terms(line, core)
+        pl.when(line > 0)(lambda: value_join(line - 1))
+
+    each(0, z + 1, value_parts)
 
     for copy in hop1_all():
         copy.wait_send()

time: 55.8 us -> 55.6 us (level)
  no operation moved by 1% of the time
where the time goes in v2:
time: 55.6 us; the launch traced here: 55.3 us
  Pallas kernels  54 us (97%)
  local copies, waits for them, and re-layouts  0.68 us (1%)
  between operations  0.64 us (1%)
    pallas_call x1, Pallas kernels, shards(): pl.pallas_call(functools.partial(kernel, heads, ctxs, group), out_shape=p...  54 us

profile of v2, /device:TPU:37, one launch (start us, length us, event | category | flops | bytes accessed | tf_op | source)
XLA Modules:
  0.0 55.3 jit_solution(3569937047272815760)
XLA Ops:
  0.6 54.0 %attention_backward.1 = bf16[3,256,128]{2,1,0:T(8,128)(2,1)S(1)} custom-call(bf16[256,128]{1,0:T(8,128)(2,1)} %refs_0_.1, bf16[256,128]{1,0:T(8,128)(2,1)} %refs_1_.1, bf16[256,128]{1,0:T(8,128)(2,1)} %refs_2_.1, bf16[48,1024]{1,0:T(8,128)(2,1)} %refs_3_.1, s32[1,48]{1,0:T(1,128)} %bitcast.9, s32[2,48]{1,0:T(2,128)} %bitcast.8), custom_call_target="tpu_custom_call" | custom-call | tf_op jit(solution)/shard_map/attention_backward/pallas_call | solution.py:558
  54.6 0.7 %slice_bitcast_fusion = (bf16[256,128]{1,0:T(8,128)(2,1)}, bf16[256,128]{1,0:T(8,128)(2,1)}, bf16[256,128]{1,0:T(8,128)(2,1)}) fusion(bf16[3,256,128]{2,1,0:T(8,128)(2,1)S(1)} %attention_backward.1), kind=kLoop, calls=%fused_computation | loop fusion | bytes 393216 | tf_op jit(solution)/shard_map/squeeze | solution.py:569

commit v3 on v2

--- a/solution.py
+++ b/solution.py
@@ -242,6 +242,7 @@
     codes = [
         jnp.where(left, slots[h : h + 1], slots[h + 1 : h + 2]) for h in range(0, heads, 2)
     ]
+    wide = jnp.concatenate([teacher, first], axis=1)
     mine = lax.rem(me_c, 4) * 32
 
     def pack(step):
@@ -253,9 +254,10 @@
         wanted = jnp.where(spot < CAP, dest * CAP + spot + 128 * head, -5).astype(F32)
         chosen = [(wanted == code).astype(F32).astype(BF16) for code in codes]
         chosen = jnp.concatenate(chosen, axis=1)
-        moved = dot_nn(chosen, teacher).reshape(8, 32, DH)
+        both = dot_nn(chosen, wide)
+        moved = both[:, 0:DH].reshape(8, 32, DH)
         diagonal = (iota((256, DH), 1) == within + mine).astype(F32)
-        lower = (dot_nn(chosen, first) * diagonal).reshape(8, 32, DH)
+        lower = (both[:, DH : 2 * DH] * diagonal).reshape(8, 32, DH)
         upper = (dot_nn(chosen, last) * diagonal).reshape(8, 32, DH)
         lower = jnp.sum(lower, axis=1, keepdims=True)
         upper = jnp.sum(upper, axis=1, keepdims=True)

time: 55.6 us -> 55.4 us (level)
  no operation moved by 1% of the time
where the time goes in v3:
time: 55.4 us; the launch traced here: 55.3 us
  Pallas kernels  54 us (97%)
  local copies, waits for them, and re-layouts  0.68 us (1%)
  between operations  0.64 us (1%)
    pallas_call x1, Pallas kernels, shards(): pl.pallas_call(functools.partial(kernel, heads, ctxs, group), out_shape=p...  54 us

profile of v3, /device:TPU:37, one launch (start us, length us, event | category | flops | bytes accessed | tf_op | source)
XLA Modules:
  0.0 55.3 jit_solution(8782841786657431481)
XLA Ops:
  0.6 54.0 %attention_backward.1 = bf16[3,256,128]{2,1,0:T(8,128)(2,1)S(1)} custom-call(bf16[256,128]{1,0:T(8,128)(2,1)} %refs_0_.1, bf16[256,128]{1,0:T(8,128)(2,1)} %refs_1_.1, bf16[256,128]{1,0:T(8,128)(2,1)} %refs_2_.1, bf16[48,1024]{1,0:T(8,128)(2,1)} %refs_3_.1, s32[1,48]{1,0:T(1,128)} %bitcast.9, s32[2,48]{1,0:T(2,128)} %bitcast.8), custom_call_target="tpu_custom_call" | custom-call | tf_op jit(solution)/shard_map/attention_backward/pallas_call | solution.py:560
  54.6 0.7 %slice_bitcast_fusion = (bf16[256,128]{1,0:T(8,128)(2,1)}, bf16[256,128]{1,0:T(8,128)(2,1)}, bf16[256,128]{1,0:T(8,128)(2,1)}) fusion(bf16[3,256,128]{2,1,0:T(8,128)(2,1)S(1)} %attention_backward.1), kind=kLoop, calls=%fused_computation | loop fusion | bytes 393216 | tf_op jit(solution)/shard_map/squeeze | solution.py:571
